TPU v7x, 32 devices: a whole 2x2x4 slice. The times are simulated.
32 devices in a mesh: tile: 4 (over y, core), rep: 8 (over z, x).
Axes of the slice: x: 2, y: 2, z: 4, core: 2. Of those that a mesh axis runs over, the one named last changes fastest.
Arguments:
- inputs: bfloat16 [8, 8, 32, 32, 256], P('rep', 'tile'), may hold values from -6 to 6
- grad_out: bfloat16 [8, 8, 32, 32, 256], P('rep', 'tile'), may hold values from -6 to 6
- seam_links: int32 [8, 4, 3], P('tile'), may hold values from 0 to 7, as said below
- corner_links: int32 [8, 4, 2], P('tile'), may hold values from 0 to 7, as said below
- dw_weight: float32 [256, 9], replicated, may hold values from -1 to 1
- norm_gain: float32 [256], replicated, may hold values from 0.1 to 1.9
- w_in: bfloat16 [256, 1024], replicated, may hold values from -0.375 to 0.375
- bias_in: float32 [1024], replicated, may hold values from -1 to 1
- w_out: bfloat16 [1024, 256], replicated, may hold values from -0.1875 to 0.1875
- layer_scale: float32 [256], replicated, may hold values from 0.25 to 2
Outputs:
- block_out: bfloat16 [8, 8, 32, 32, 256], P('rep', 'tile')
- x_grad: float32 [8, 8, 32, 32, 256], P('rep', 'tile')
- grad_dw: float32 [256, 9], replicated
- grad_gain: float32 [256], replicated
- grad_w_in: float32 [256, 1024], replicated
- grad_bias: float32 [1024], replicated
- grad_w_out: float32 [1024, 256], replicated
- grad_scale: float32 [256], replicated
Inputs may be any that keep to these rules, and one draw needn't show every extreme that they name: `seam_links`: entry [t, s] = (t2, s2, f): side s of tile t meets side s2 of tile t2, reversed if f = 1. Sides are paired: entry [t2, s2] = (t, s, f), and no entry names its own side. `corner_links`: entry [t, k] = (t2, k2): corner k of tile t meets corner k2 of tile t2. Corners are paired: entry [t2, k2] = (t, k), and no entry names its own corner.
All inputs are finite; a program needn't handle non-finite values.
Results may differ from a plain program's by a relative error of at most 0.0063.
Values may be sent and summed in bfloat16 or wider, within the bound.
A program may use at most 64 MiB of HBM per device.

v0:
```python
import math
import jax
import jax.numpy as jnp
from jax import lax
from jax.sharding import PartitionSpec as P

INV_ROOT_TWO = 0.7071067811865476
INV_ROOT_TAU = 0.3989422804014327


def edge_strips(blocks):
    top_row = blocks[..., 0, :, :]
    right_col = blocks[..., :, -1, :]
    bottom_row = blocks[..., -1, ::-1, :]
    left_col = blocks[..., ::-1, 0, :]
    return jnp.stack([top_row, right_col, bottom_row, left_col], axis=-3)


def corner_cells(blocks):
    return jnp.stack(
        [
            blocks[..., 0, 0, :],
            blocks[..., 0, -1, :],
            blocks[..., -1, -1, :],
            blocks[..., -1, 0, :],
        ],
        axis=-2,
    )


def fetch_linked(all_strips, all_points, seam_links, corner_links):
    picked = all_strips[:, seam_links[..., 0], seam_links[..., 1]]
    reverse = (seam_links[..., 2] == 1)[None, :, :, None, None]
    strips = jnp.where(reverse, picked[..., ::-1, :], picked)
    points = all_points[:, corner_links[..., 0], corner_links[..., 1]]
    return (strips, points)


def assemble(blocks, strips, points):
    top_row = jnp.concatenate(
        [points[..., 0:1, :], strips[..., 0, :, :], points[..., 1:2, :]], axis=-2
    )
    bottom_row = jnp.concatenate(
        [points[..., 3:4, :], strips[..., 2, ::-1, :], points[..., 2:3, :]], axis=-2
    )
    left_col = strips[..., 3, ::-1, :][..., :, None, :]
    right_col = strips[..., 1, :, :][..., :, None, :]
    middle = jnp.concatenate([left_col, blocks, right_col], axis=-2)
    return jnp.concatenate([top_row[..., None, :, :], middle, bottom_row[..., None, :, :]], axis=-3)


def padded_parts(grad_padded):
    interior = grad_padded[..., 1:-1, 1:-1, :]
    top_row = grad_padded[..., 0, 1:-1, :]
    right_col = grad_padded[..., 1:-1, -1, :]
    bottom_row = grad_padded[..., -1, 1:-1, :][..., ::-1, :]
    left_col = grad_padded[..., 1:-1, 0, :][..., ::-1, :]
    strips = jnp.stack([top_row, right_col, bottom_row, left_col], axis=-3)
    points = jnp.stack(
        [
            grad_padded[..., 0, 0, :],
            grad_padded[..., 0, -1, :],
            grad_padded[..., -1, -1, :],
            grad_padded[..., -1, 0, :],
        ],
        axis=-2,
    )
    return (interior, strips, points)


def add_to_rims(target, strips, points):
    extent = target.shape[-2]
    row_ids = lax.broadcasted_iota(jnp.int32, (extent, 1, 1), 0)
    col_ids = lax.broadcasted_iota(jnp.int32, (1, extent, 1), 1)
    top_mask = row_ids == 0
    bottom_mask = row_ids == extent - 1
    left_mask = col_ids == 0
    right_mask = col_ids == extent - 1
    target = target + jnp.where(top_mask, strips[..., 0, :, :][..., None, :, :], 0.0)
    target = target + jnp.where(right_mask, strips[..., 1, :, :][..., :, None, :], 0.0)
    target = target + jnp.where(bottom_mask, strips[..., 2, ::-1, :][..., None, :, :], 0.0)
    target = target + jnp.where(left_mask, strips[..., 3, ::-1, :][..., :, None, :], 0.0)
    target = target + jnp.where(top_mask & left_mask, points[..., 0, :][..., None, None, :], 0.0)
    target = target + jnp.where(top_mask & right_mask, points[..., 1, :][..., None, None, :], 0.0)
    target = target + jnp.where(
        bottom_mask & right_mask, points[..., 2, :][..., None, None, :], 0.0
    )
    target = target + jnp.where(bottom_mask & left_mask, points[..., 3, :][..., None, None, :], 0.0)
    return target


def forward_backward(
    padded, blocks, grad_out, dw_weight, norm_gain, w_in, bias_in, w_out, layer_scale
):
    extent = blocks.shape[-2]
    channels = blocks.shape[-1]
    mixed_cells = jnp.zeros(blocks.shape, jnp.float32)
    for row_off in range(3):
        for col_off in range(3):
            tap_index = 3 * row_off + col_off
            window = padded[..., row_off : row_off + extent, col_off : col_off + extent, :].astype(
                jnp.float32
            )
            mixed_cells = mixed_cells + window * dw_weight[:, tap_index]
    average = jnp.mean(mixed_cells, axis=-1, keepdims=True)
    centred = mixed_cells - average
    inv_std = lax.rsqrt(jnp.mean(centred * centred, axis=-1, keepdims=True) + 1e-06)
    standard = centred * inv_std
    normed = (standard * norm_gain).astype(jnp.bfloat16).reshape(-1, channels)
    hidden_pre = jnp.dot(normed, w_in, preferred_element_type=jnp.float32) + bias_in
    activated = jax.nn.gelu(hidden_pre, approximate=False).astype(jnp.bfloat16)
    branch = jnp.dot(activated, w_out, preferred_element_type=jnp.float32)
    cotangent = grad_out.reshape(-1, channels).astype(jnp.float32)
    block_out = (
        (blocks.reshape(-1, channels).astype(jnp.float32) + layer_scale * branch)
        .astype(jnp.bfloat16)
        .reshape(blocks.shape)
    )
    grad_scale = jnp.sum(cotangent * branch, axis=0)
    grad_mix = (cotangent * layer_scale).astype(jnp.bfloat16)
    grad_w_out = lax.dot_general(
        activated, grad_mix, (((0,), (0,)), ((), ())), preferred_element_type=jnp.float32
    )
    grad_act = lax.dot_general(
        grad_mix, w_out, (((1,), (1,)), ((), ())), preferred_element_type=jnp.float32
    )
    gelu_slope = (
        0.5 * (1.0 + lax.erf(hidden_pre * INV_ROOT_TWO))
        + hidden_pre * jnp.exp(-0.5 * hidden_pre * hidden_pre) * INV_ROOT_TAU
    )
    grad_hidden = (grad_act * gelu_slope).astype(jnp.bfloat16)
    grad_bias = jnp.sum(grad_hidden.astype(jnp.float32), axis=0)
    grad_w_in = lax.dot_general(
        normed, grad_hidden, (((0,), (0,)), ((), ())), preferred_element_type=jnp.float32
    )
    grad_normed = lax.dot_general(
        grad_hidden, w_in, (((1,), (1,)), ((), ())), preferred_element_type=jnp.float32
    ).reshape(blocks.shape)
    grad_gain = jnp.sum((grad_normed * standard).reshape(-1, channels), axis=0)
    grad_unit = grad_normed * norm_gain
    grad_mixed = (
        grad_unit
        - jnp.mean(grad_unit, axis=-1, keepdims=True)
        - standard * jnp.mean(grad_unit * standard, axis=-1, keepdims=True)
    ) * inv_std
    pad_widths = [(0, 0)] * (grad_mixed.ndim - 3) + [(2, 2), (2, 2), (0, 0)]
    wide_grad = jnp.pad(grad_mixed, pad_widths)
    grad_padded = jnp.zeros(padded.shape, jnp.float32)
    dw_columns = []
    for row_off in range(3):
        for col_off in range(3):
            tap_index = 3 * row_off + col_off
            window = padded[..., row_off : row_off + extent, col_off : col_off + extent, :].astype(
                jnp.float32
            )
            shifted = wide_grad[
                ..., 2 - row_off : 4 - row_off + extent, 2 - col_off : 4 - col_off + extent, :
            ]
            grad_padded = grad_padded + shifted * dw_weight[:, tap_index]
            dw_columns.append(jnp.sum((grad_mixed * window).reshape(-1, channels), axis=0))
    grad_dw = jnp.stack(dw_columns, axis=1)
    return (
        block_out,
        grad_padded,
        (grad_dw, grad_gain, grad_w_in, grad_bias, grad_w_out, grad_scale),
    )


def body(
    inputs,
    grad_out,
    seam_links,
    corner_links,
    dw_weight,
    norm_gain,
    w_in,
    bias_in,
    w_out,
    layer_scale,
):
    all_strips, all_points = (
        lax.all_gather(edge_strips(inputs), "tile", axis=1, tiled=True),
        lax.all_gather(corner_cells(inputs), "tile", axis=1, tiled=True),
    )
    strips, points = fetch_linked(all_strips, all_points, seam_links, corner_links)
    padded = assemble(inputs, strips, points)
    block_out, grad_padded, partials = forward_backward(
        padded, inputs, grad_out, dw_weight, norm_gain, w_in, bias_in, w_out, layer_scale
    )
    grad_dw, grad_gain, grad_w_in, grad_bias, grad_w_out, grad_scale = partials
    interior, back_strips, back_points = padded_parts(grad_padded)
    home_strips, home_points = (
        lax.all_gather(back_strips.astype(jnp.bfloat16), "tile", axis=1, tiled=True).astype(
            back_strips.dtype
        ),
        lax.all_gather(back_points.astype(jnp.bfloat16), "tile", axis=1, tiled=True).astype(
            back_points.dtype
        ),
    )
    return_strips, return_points = fetch_linked(home_strips, home_points, seam_links, corner_links)
    x_grad = add_to_rims(grad_out.astype(jnp.float32) + interior, return_strips, return_points)
    cell_total = (
        lax.axis_size("tile")
        * lax.axis_size("rep")
        * inputs.shape[0]
        * inputs.shape[1]
        * inputs.shape[2]
        * inputs.shape[3]
    )
    factor = 1.0 / math.sqrt(cell_total)
    summed = lax.psum(
        (grad_dw, grad_gain, grad_w_in, grad_bias, grad_w_out, grad_scale), ("tile", "rep")
    )
    return (
        block_out,
        x_grad,
        summed[0] * factor,
        summed[1] * factor,
        summed[2] * factor,
        summed[3] * factor,
        summed[4] * factor,
        summed[5] * factor,
    )


def solution(mesh):
    placed = (
        P("rep", "tile", None, None, None),
        P("rep", "tile", None, None, None),
        P("tile", None, None),
        P("tile", None, None),
        P(),
        P(),
        P(),
        P(),
        P(),
        P(),
    )
    return jax.shard_map(
        body,
        mesh=mesh,
        in_specs=placed,
        out_specs=(
            P("rep", "tile", None, None, None),
            P("rep", "tile", None, None, None),
            P(),
            P(),
            P(),
            P(),
            P(),
            P(),
        ),
        check_vma=False,
    )
```

profile of v0, /device:TPU:0, one launch (start us, length us, event | category | flops | bytes accessed | tf_op | source)
XLA Modules:
  0.0 216.6 jit_solution(4268885214619424398)
XLA Ops:
  8.1 1.1 fusion.75
  11.5 6.2 %all_gather.12 = bf16[1,8,4,256]{3,2,0,1:T(4,128)(2,1)S(1)} all-gather(bf16[1,2,4,256]{3,2,0,1:T(4,128)(2,1)S(1)} %copy.212), channel_id=1, replica_groups=mesh['tile'=4,'rep'=8] {'tile'}, dimensions={1}, use_global_device_ids=true | all-gather | bytes 20480 | tf_op jit(solution)/shard_map/all_gather | solution.py:183
  19.4 7.6 %all_gather.13 = bf16[1,8,4,32,256]{4,3,1,2,0:T(8,128)(2,1)S(1)} all-gather(bf16[1,2,4,32,256]{4,3,1,2,0:T(8,128)(2,1)S(1)} %pad_maximum_fusion.3), channel_id=1, replica_groups=mesh['tile'=4,'rep'=8] {'tile'}, dimensions={1}, use_global_device_ids=true | all-gather | bytes 655360 | tf_op jit(solution)/shard_map/all_gather | solution.py:182
  28.4 1.7 maximum_maximum_fusion
  30.1 5.2 %fusion.72 = (f32[2,32,32]{2,1,0:T(8,128)S(1)}, f32[1,2,32,32,256]{4,3,2,1,0:T(8,128)S(1)}) fusion(f32[256]{0:T(256)S(1)} %bitcast.170, bf16[1,2,33,34,256]{4,3,2,1,0:T(8,128)(2,1)S(1)} %get-tuple-element.81, f32[256]{0:T(256)S(1)} %bitcast.172, f32[256]{0:T(256)S(1)} %bitcast.158, f32[256]{0:T(256)S(1)} %bitcast.160, ...), kind=kLoop, calls=%fused_computation.185 | loop fusion | flops 17299456 | bytes 9520128 | tf_op jit(solution)/shard_map/reduce_sum | solution.py:105
  36.8 19.3 %fusion.2 = (bf16[2048,1024]{1,0:T(8,128)(2,1)S(1)}, f32[2048,1024]{1,0:T(8,128)S(1)}) fusion(f32[1024]{0:T(1024)S(1)} %copy-done.13, bf16[2048,256]{1,0:T(8,128)(2,1)S(1)} %bitcast.144, bf16[256,1024]{1,0:T(8,128)(2,1)S(1)} %copy-done), kind=kOutput, calls=%fused_computation.8 | convolution fusion | flops 1212153856 | bytes 14159872 | tf_op jit(solution)/shard_map/dot_general | solution.py:110
  56.2 3.1 %fusion.58 = (f32[256]{0:T(256)}, bf16[2048,256]{1,0:T(8,128)(2,1)}, bf16[2048,256]{1,0:T(8,128)(2,1)S(1)}) fusion(bf16[1,2,32,32,256]{4,3,2,1,0:T(8,128)(2,1)S(1)} %copy-done.6, f32[256]{0:T(256)S(1)} %copy-done.14, bf16[1,2,32,32,256]{4,3,2,1,0:T(8,128)(2,1)S(1)} %copy-done.5, bf16[2048,1024]{1,0:T(8,128)(2,1)S(1)} %get-tuple-element.122, ...), kind=kOutput, calls=%fused_computation.102 | convolution fusion | flops 1078460160 | bytes 8914944 | tf_op jit(solution)/shard_map/dot_general | solution.py:112
  59.3 2.2 %fusion.82 = f32[1024,256]{1,0:T(8,128)} fusion(bf16[2048,1024]{1,0:T(8,128)(2,1)S(1)} %get-tuple-element.122, bf16[2048,256]{1,0:T(8,128)(2,1)S(1)} %get-tuple-element.82), kind=kOutput, calls=%fused_computation.194 | convolution fusion | flops 1073741824 | bytes 6291456 | tf_op jit(solution)/shard_map/dot_general | solution.py:121
  61.5 4.9 %convert_reduce_fusion = (f32[1024]{0:T(1024)S(1)}, bf16[2048,1024]{1,0:T(8,128)(2,1)S(1)}) fusion(f32[2048,1024]{1,0:T(8,128)S(1)} %get-tuple-element.123, f32[1024]{0:T(1024)S(1)} %copy-done.13, bf16[2048,256]{1,0:T(8,128)(2,1)S(1)} %get-tuple-element.82, bf16[1024,256]{1,0:T(8,128)(2,1)S(1)} %copy-done.12), kind=kOutput, calls=%fused_computation.15 | convolution fusion | flops 1101003776 | bytes 14163968 | tf_op jit(solution)/shard_map/dot_general | solution.py:124
  66.4 1.9 copy-done.15
  68.3 2.2 %fusion.81 = f32[256,1024]{1,0:T(8,128)} fusion(bf16[2048,256]{1,0:T(8,128)(2,1)S(1)} %bitcast.145, bf16[2048,1024]{1,0:T(8,128)(2,1)S(1)} %get-tuple-element.127), kind=kOutput, calls=%fused_computation.193 | convolution fusion | flops 1073741824 | bytes 6291456 | tf_op jit(solution)/shard_map/dot_general | solution.py:133
  70.6 3.6 %multiply_reduce_fusion.3 = (f32[2048]{0:T(1024)S(1)}, f32[2048,256]{1,0:T(8,128)S(1)}) fusion(f32[256]{0:T(256)S(1)} %copy-done.9, bf16[2048,1024]{1,0:T(8,128)(2,1)} %copy-done.15, bf16[256,1024]{1,0:T(8,128)(2,1)S(1)} %copy-done), kind=kOutput, calls=%fused_computation.109 | convolution fusion | flops 1074788352 | bytes 6824960 | tf_op jit(solution)/shard_map/dot_general | solution.py:136
  74.2 1.1 multiply_reduce_fusion
  75.6 8.3 %fusion.48 = (f32[256]{0:T(256)S(1)}, f32[256]{0:T(256)S(1)}, f32[256]{0:T(256)S(1)}, f32[256]{0:T(256)S(1)}, f32[256]{0:T(256)S(1)}, /*index=5*/f32[256]{0:T(25...) fusion(bf16[1,2,33,34,256]{4,3,2,1,0:T(8,128)(2,1)} %copy-done.2, ...), kind=kLoop, calls=%fused_computation.89 | loop fusion | flops 20969216 | bytes 13740032 | tf_op jit(solution)/shard_map/reduce_sum | solution.py:160
  83.9 2.8 %fusion.24 = f32[1,2,34,34,256]{4,3,2,1,0:T(8,128)S(1)} fusion(f32[1,2,32,32,256]{4,3,2,1,0:T(8,128)S(1)} %get-tuple-element.71, f32[256]{0:T(256)S(1)} %bitcast.171, f32[256]{0:T(256)S(1)} %bitcast.173, f32[256]{0:T(256)S(1)} %bitcast.159, f32[256]{0:T(256)S(1)} %bitcast.161, f32[256]{0:T(256)S(1)} %bitcast.163, f32[256]{0:T(256)S(1)} %bitcast.165, ...), kind=kLoop, calls=%fused_computation.48 | loop fusion | flops 10061824 | bytes 4473856 | tf_op jit(solution)/shard_map/add | solution.py:159
  88.7 40.9 %all-reduce.1 = (f32[256,9]{0,1:T(8,128)}, f32[256]{0:T(256)S(1)}, f32[1024]{0:T(1024)S(1)}, f32[256]{0:T(256)S(1)}) all-reduce(f32[256,9]{0,1:T(8,128)S(1)} %stack.78, f32[256]{0:T(256)S(1)} %get-tuple-element.57, f32[1024]{0:T(1024)S(1)} %get-tuple-element.126, ...), channel_id=1, replica_groups=mesh['tile'=4,'rep'=8] {'tile','rep'}, use_global_device_ids=true, to_apply=%region_13.14 | all-reduce | flops 3840 | bytes 30720 | tf_op jit(solution)/shard_map/psum | solution.py:211
  132.4 8.5 %all_gather.14 = bf16[1,8,4,32,256]{4,3,2,0,1:T(8,128)(2,1)S(1)} all-gather(bf16[1,2,4,32,256]{4,3,2,0,1:T(8,128)(2,1)S(1)} %copy.228), channel_id=1, replica_groups=mesh['tile'=4,'rep'=8] {'tile'}, dimensions={1}, use_global_device_ids=true | all-gather | bytes 655360 | tf_op jit(solution)/shard_map/all_gather | solution.py:193
  142.0 2.5 %gather_fusion.2 = f32[8,32,256]{2,1,0:T(8,128)} fusion(f32[8,4,32,256]{3,2,1,0:T(8,128)} %bitcast_convert_fusion, s32[8]{0:T(128)S(1)} %reshape.484), kind=kCustom, calls=%fused_computation.2 | custom fusion | bytes 524352 | tf_op jit(solution)/shard_map/gather | solution.py:32
  144.5 1.6 rev.37
  146.1 1.1 broadcast_select_fusion
  148.6 5.2 %all_gather.15 = bf16[1,8,4,256]{3,2,0,1:T(4,128)(2,1)S(1)} all-gather(bf16[1,2,4,256]{3,2,0,1:T(4,128)(2,1)S(1)} %copy.230), channel_id=1, replica_groups=mesh['tile'=4,'rep'=8] {'tile'}, dimensions={1}, use_global_device_ids=true | all-gather | bytes 20480 | tf_op jit(solution)/shard_map/all_gather | solution.py:196
  156.0 4.5 %fusion.56 = f32[1,2,32,32,256]{4,3,2,1,0:T(8,128)} fusion(f32[1,2,34,34,256]{4,3,2,1,0:T(8,128)S(1)} %fusion.24, bf16[1,2,32,32,256]{4,3,2,1,0:T(8,128)(2,1)} %param.11, f32[2,256]{1,0:T(2,128)S(1)} %bitcast.174, f32[2,256]{1,0:T(2,128)S(1)} %bitcast.175, f32[2,256]{1,0:T(2,128)S(1)} %bitcast.176, f32[2,256]{1,0:T(2,128)S(1)} %bitcast.177, ...), kind=kLoop, calls=%fused_computation.98 | loop fusion | flops 9437184 | bytes 5531648 | tf_op jit(solution)/shard_map/add | solution.py:88
  160.5 45.8 %all-reduce.5.cloned.1.call-done = (f32[256,1024]{1,0:T(8,128)}, f32[1024,256]{1,0:T(8,128)}) async-done(((f32[256,1024]{1,0:T(8,128)}, f32[1024,256]{1,0:T(8,128)}), (f32[256,1024]{1,0:T(8,128)}, f32[1024,256]{1,0:T(8,128)})) %all-reduce.5.cloned.1.call-update) | async-done | bytes 2097168 | tf_op jit(solution)/shard_map/psum | solution.py:211
  206.3 2.4 %broadcast_multiply_fusion = f32[1024,256]{1,0:T(8,128)} fusion(f32[1024,256]{1,0:T(8,128)} %get-tuple-element.70), kind=kLoop, calls=%fused_computation.118 | loop fusion | flops 262144 | bytes 2097152 | tf_op jit(solution)/shard_map/mul | solution.py:221
  (109 shorter events, 18.1 us)
Async XLA Ops:
  7.2 29.6 %copy-start = (bf16[256,1024]{1,0:T(8,128)(2,1)S(1)}, bf16[256,1024]{1,0:T(8,128)(2,1)}, u32[]{:S(2)}) copy-start(bf16[256,1024]{1,0:T(8,128)(2,1)} %param.16) | copy-start | bytes 1572868
  7.2 21.2 %copy-start.4 = (bf16[1,2,32,32,256]{4,3,2,1,0:T(8,128)(2,1)S(1)}, bf16[1,2,32,32,256]{4,3,2,1,0:T(8,128)(2,1)}, u32[]{:S(2)}) copy-start(bf16[1,2,32,32,256]{4,3,2,1,0:T(8,128)(2,1)} %param.10) | copy-start | bytes 3145732
  7.2 21.1 %copy-start.10 = (f32[256,9]{0,1:T(8,128)S(1)}, f32[256,9]{0,1:T(8,128)}, u32[]{:S(2)}) copy-start(f32[256,9]{0,1:T(8,128)} %param.14) | copy-start | bytes 27652
  7.2 199.1 %all-reduce.5.cloned.1.call-start = ((), (), s32[]{:S(2)}) async-start(), calls=%async_computation | async-start | bytes 4194304 | tf_op jit(solution)/shard_map/psum | solution.py:211
  11.4 16.4 %copy-start.11 = (pred[2,4]{1,0:T(4,128)(4,1)}, pred[2,4]{1,0:T(4,128)(4,1)S(1)}, u32[]{:S(2)}) copy-start(pred[2,4]{1,0:T(4,128)(4,1)S(1)} %compare_bitcast_fusion) | copy-start | bytes 28
  30.1 5.2 %copy-start.1 = (bf16[1,2,33,34,256]{4,3,2,1,0:T(8,128)(2,1)}, bf16[1,2,33,34,256]{4,3,2,1,0:T(8,128)(2,1)S(1)}, u32[]{:S(2)}) copy-start(bf16[1,2,33,34,256]{4,3,2,1,0:T(8,128)(2,1)S(1)} %get-tuple-element.80) | copy-start | bytes 3446788
  30.1 5.2 %copy-start.2 = (bf16[1,2,33,34,256]{4,3,2,1,0:T(8,128)(2,1)}, bf16[1,2,33,34,256]{4,3,2,1,0:T(8,128)(2,1)S(1)}, u32[]{:S(2)}) copy-start(bf16[1,2,33,34,256]{4,3,2,1,0:T(8,128)(2,1)S(1)} %get-tuple-element.81) | copy-start | bytes 3446788
  30.1 5.9 %copy-start.9 = (f32[256]{0:T(256)S(1)}, f32[256]{0:T(256)}, u32[]{:S(2)}) copy-start(f32[256]{0:T(256)} %param.15) | copy-start | bytes 3076
  35.3 1.4 copy-start.13
  36.8 19.4 %copy-start.5 = (bf16[1,2,32,32,256]{4,3,2,1,0:T(8,128)(2,1)S(1)}, bf16[1,2,32,32,256]{4,3,2,1,0:T(8,128)(2,1)}, u32[]{:S(2)}) copy-start(bf16[1,2,32,32,256]{4,3,2,1,0:T(8,128)(2,1)} %param.10) | copy-start | bytes 3145732
  36.8 19.4 %copy-start.6 = (bf16[1,2,32,32,256]{4,3,2,1,0:T(8,128)(2,1)S(1)}, bf16[1,2,32,32,256]{4,3,2,1,0:T(8,128)(2,1)}, u32[]{:S(2)}) copy-start(bf16[1,2,32,32,256]{4,3,2,1,0:T(8,128)(2,1)} %param.11) | copy-start | bytes 3145732
  36.8 19.4 %copy-start.12 = (bf16[1024,256]{1,0:T(8,128)(2,1)S(1)}, bf16[1024,256]{1,0:T(8,128)(2,1)}, u32[]{:S(2)}) copy-start(bf16[1024,256]{1,0:T(8,128)(2,1)} %param.18) | copy-start | bytes 1572868
  36.8 19.4 %copy-start.14 = (f32[256]{0:T(256)S(1)}, f32[256]{0:T(256)}, u32[]{:S(2)}) copy-start(f32[256]{0:T(256)} %param.19) | copy-start | bytes 3076
  66.4 1.9 copy-start.15
  74.2 1.3 copy-start.3
  132.3 23.1 %copy-start.8 = (f32[256,9]{0,1:T(8,128)S(1)}, f32[256,9]{0,1:T(8,128)}, u32[]{:S(2)}) copy-start(f32[256,9]{0,1:T(8,128)} %get-tuple-element.65) | copy-start | bytes 27652
  206.3 2.4 %copy-start.7 = (f32[256,1024]{1,0:T(8,128)S(1)}, f32[256,1024]{1,0:T(8,128)}, u32[]{:S(2)}) copy-start(f32[256,1024]{1,0:T(8,128)} %get-tuple-element.69) | copy-start | bytes 3145732
Sparse Core Ops, SparseCore 0:
  70.7 135.4 all-reduce.4
where the time goes:
time: 217 us
  blocking collectives  68.5 us (32%)
  waiting for transfers between devices  45.8 us (21%)
  other arithmetic  35.4 us (16%)
  matrix products  35.4 us (16%)
  local copies, waits for them, and re-layouts  16.8 us (8%)
  between operations  14.6 us (7%)
    psum x1, waiting for transfers between devices, body(): lax.psum((grad_dw, grad_gain, grad_w_in, grad_bias, grad_w_out, grad_scal...  45.8 us
    psum x1, blocking collectives, body(): lax.psum((grad_dw, grad_gain, grad_w_in, grad_bias, grad_w_out, grad_scal...  40.9 us
    dot_general x1, matrix products, forward_backward(): jnp.dot(normed, w_in, preferred_element_type=jnp.float32) + bias_in  19.3 us
    all_gather x1, blocking collectives, body(): lax.all_gather(back_strips.astype(jnp.bfloat16), 'tile', axis=1, tiled=True)  8.53 us
    reduce_sum x1, other arithmetic, forward_backward(): jnp.sum((grad_mixed * window).reshape(-1, channels), axis=0)  8.32 us
    all_gather x1, blocking collectives, body(): lax.all_gather(edge_strips(inputs), 'tile', axis=1, tiled=True)  7.62 us
    all_gather x1, blocking collectives, body(): lax.all_gather(corner_cells(inputs), 'tile', axis=1, tiled=True)  6.22 us
    all_gather x1, blocking collectives, body(): lax.all_gather(back_points.astype(jnp.bfloat16), 'tile', axis=1, tiled=True)  5.19 us
  transfers between devices with their start and end apart: 1, of which 1 were waited for; matrix products, arithmetic and copies ran while one was open for 16% of the time, Pallas kernels for 0%

commit v1 on v0

--- a/solution.py
+++ b/solution.py
@@ -6,6 +6,26 @@
 
 INV_ROOT_TWO = 0.7071067811865476
 INV_ROOT_TAU = 0.3989422804014327
+
+
+def _edit_sites(load, in_dim):
+    load = jnp.moveaxis(load, 0, in_dim)
+    odd = load.shape
+    return load.reshape(*odd[:in_dim], odd[in_dim] * odd[in_dim + 1], *odd[in_dim + 2 :])
+
+
+def arrange_spans(sample, axis_id):
+    all_rows = sample[None]
+    dev_count = lax.axis_size(axis_id)
+    for p in range(dev_count.bit_length() - 1):
+        local_next = 1 << p
+        now = lax.ppermute(
+            all_rows, axis_id, tuple(((w, w ^ local_next) for w in range(dev_count)))
+        )
+        opened = jnp.stack([all_rows, now], 0)
+        earlier = lax.axis_index(axis_id) >> p & 1
+        all_rows = jnp.where(earlier == 0, opened, opened[::-1]).reshape(-1, *sample.shape)
+    return all_rows
 
 
 def edge_strips(blocks):
@@ -178,6 +198,11 @@
     w_out,
     layer_scale,
 ):
+
+    def lift_the_zone(x_part, block_in, axis_k):
+        view_out = arrange_spans(x_part, block_in)
+        return _edit_sites(view_out, axis_k)
+
     all_strips, all_points = (
         lax.all_gather(edge_strips(inputs), "tile", axis=1, tiled=True),
         lax.all_gather(corner_cells(inputs), "tile", axis=1, tiled=True),
@@ -193,9 +218,7 @@
         lax.all_gather(back_strips.astype(jnp.bfloat16), "tile", axis=1, tiled=True).astype(
             back_strips.dtype
         ),
-        lax.all_gather(back_points.astype(jnp.bfloat16), "tile", axis=1, tiled=True).astype(
-            back_points.dtype
-        ),
+        lift_the_zone(back_points.astype(jnp.bfloat16), "tile", 1).astype(back_points.dtype),
     )
     return_strips, return_points = fetch_linked(home_strips, home_points, seam_links, corner_links)
     x_grad = add_to_rims(grad_out.astype(jnp.float32) + interior, return_strips, return_points)

time: 217 us -> 232 us (1.069)
  waiting for transfers between devices: 45.8 us -> 65.9 us
  blocking collectives: 68.5 us -> 62.9 us
  other arithmetic: 35.4 us -> 38.2 us
    psum x1, waiting for transfers between devices: 45.8 us -> 64.4 us  [body(): lax.psum((grad_dw, grad_gain, grad_w_in, grad_bias, grad_w_out, grad_scal...]
    all_gather x1 -> x0, blocking collectives: 5.19 us -> none  [body(): lax.all_gather(back_points.astype(jnp.bfloat16), 'tile', axis=1, tiled=True)]
  transfers between devices with their start and end apart: 1 -> 3, of which waited for: 1 -> 2; matrix products, arithmetic and copies ran while one was open for 16% -> 11% of each run, Pallas kernels for 0% -> 0%
where the time goes in v1:
time: 232 us
  waiting for transfers between devices  65.9 us (28%)
  blocking collectives  62.9 us (27%)
  other arithmetic  38.2 us (16%)
  matrix products  33.8 us (15%)
  local copies, waits for them, and re-layouts  14.8 us (6%)
  between operations  14.7 us (6%)
    psum x1, waiting for transfers between devices, body(): lax.psum((grad_dw, grad_gain, grad_w_in, grad_bias, grad_w_out, grad_scal...  64.4 us
    psum x1, blocking collectives, body(): lax.psum((grad_dw, grad_gain, grad_w_in, grad_bias, grad_w_out, grad_scal...  41.3 us
    dot_general x1, matrix products, forward_backward(): jnp.dot(normed, w_in, preferred_element_type=jnp.float32) + bias_in  19.3 us
    reduce_sum x1, other arithmetic, forward_backward(): jnp.sum((grad_mixed * window).reshape(-1, channels), axis=0)  8.46 us
    all_gather x1, blocking collectives, body(): lax.all_gather(back_strips.astype(jnp.bfloat16), 'tile', axis=1, tiled=True)  7.73 us
    all_gather x1, blocking collectives, body(): lax.all_gather(edge_strips(inputs), 'tile', axis=1, tiled=True)  7.62 us
    all_gather x1, blocking collectives, body(): lax.all_gather(corner_cells(inputs), 'tile', axis=1, tiled=True)  6.22 us
    dot_general x1, matrix products, forward_backward(): lax.dot_general(grad_mix, w_out, (((1,), (1,)), ((), ())), preferred_elem...  5.46 us
  transfers between devices with their start and end apart: 3, of which 2 were waited for; matrix products, arithmetic and copies ran while one was open for 11% of the time, Pallas kernels for 0%

profile of v1, /device:TPU:0, one launch (start us, length us, event | category | flops | bytes accessed | tf_op | source)
XLA Modules:
  0.0 231.6 jit_solution(8172390650465405180)
XLA Ops:
  8.1 1.1 fusion.84
  11.5 6.2 %all_gather.9 = bf16[1,8,4,256]{3,2,0,1:T(4,128)(2,1)S(1)} all-gather(bf16[1,2,4,256]{3,2,0,1:T(4,128)(2,1)S(1)} %copy.252), channel_id=1, replica_groups=mesh['tile'=4,'rep'=8] {'tile'}, dimensions={1}, use_global_device_ids=true | all-gather | bytes 20480 | tf_op jit(solution)/shard_map/all_gather | solution.py:208
  19.4 7.6 %all_gather.10 = bf16[1,8,4,32,256]{4,3,1,2,0:T(8,128)(2,1)S(1)} all-gather(bf16[1,2,4,32,256]{4,3,1,2,0:T(8,128)(2,1)S(1)} %pad_maximum_fusion.3), channel_id=1, replica_groups=mesh['tile'=4,'rep'=8] {'tile'}, dimensions={1}, use_global_device_ids=true | all-gather | bytes 655360 | tf_op jit(solution)/shard_map/all_gather | solution.py:207
  28.4 1.7 maximum_maximum_fusion
  30.1 5.2 %fusion.82 = (f32[2,32,32]{2,1,0:T(8,128)S(1)}, f32[1,2,32,32,256]{4,3,2,1,0:T(8,128)S(1)}) fusion(f32[256]{0:T(256)S(1)} %bitcast.180, bf16[1,2,33,34,256]{4,3,2,1,0:T(8,128)(2,1)S(1)} %get-tuple-element.85, f32[256]{0:T(256)S(1)} %bitcast.182, f32[256]{0:T(256)S(1)} %bitcast.168, f32[256]{0:T(256)S(1)} %bitcast.170, ...), kind=kLoop, calls=%fused_computation.199 | loop fusion | flops 17299456 | bytes 9520128 | tf_op jit(solution)/shard_map/reduce_sum | solution.py:125
  36.8 19.3 %fusion.2 = (bf16[2048,1024]{1,0:T(8,128)(2,1)S(1)}, f32[2048,1024]{1,0:T(8,128)S(1)}) fusion(f32[1024]{0:T(1024)S(1)} %copy-done.19, bf16[2048,256]{1,0:T(8,128)(2,1)S(1)} %bitcast.154, bf16[256,1024]{1,0:T(8,128)(2,1)S(1)} %copy-done), kind=kOutput, calls=%fused_computation.8 | convolution fusion | flops 1212153856 | bytes 14159872 | tf_op jit(solution)/shard_map/dot_general | solution.py:130
  56.2 3.1 %fusion.58 = (f32[256]{0:T(256)}, bf16[2048,256]{1,0:T(8,128)(2,1)}, bf16[2048,256]{1,0:T(8,128)(2,1)S(1)}) fusion(bf16[1,2,32,32,256]{4,3,2,1,0:T(8,128)(2,1)S(1)} %copy-done.6, f32[256]{0:T(256)S(1)} %copy-done.20, bf16[1,2,32,32,256]{4,3,2,1,0:T(8,128)(2,1)S(1)} %copy-done.5, bf16[2048,1024]{1,0:T(8,128)(2,1)S(1)} %get-tuple-element.128, ...), kind=kOutput, calls=%fused_computation.102 | convolution fusion | flops 1078460160 | bytes 8914944 | tf_op jit(solution)/shard_map/dot_general | solution.py:132
  59.3 5.5 %convert_reduce_fusion = (f32[1024]{0:T(1024)}, bf16[2048,1024]{1,0:T(8,128)(2,1)S(1)}) fusion(f32[2048,1024]{1,0:T(8,128)S(1)} %get-tuple-element.129, f32[1024]{0:T(1024)S(1)} %copy-done.19, bf16[2048,256]{1,0:T(8,128)(2,1)S(1)} %get-tuple-element.86, bf16[1024,256]{1,0:T(8,128)(2,1)S(1)} %copy-done.18), kind=kOutput, calls=%fused_computation.15 | convolution fusion | flops 1101003776 | bytes 14163968 | tf_op jit(solution)/shard_map/dot_general | solution.py:144
  64.8 1.4 multiply_reduce_fusion.3
  68.1 8.5 %fusion.48 = (f32[256]{0:T(256)S(1)}, f32[256]{0:T(256)S(1)}, f32[256]{0:T(256)S(1)}, f32[256]{0:T(256)S(1)}, f32[256]{0:T(256)S(1)}, /*index=5*/f32[256]{0:T(25...) fusion(bf16[1,2,33,34,256]{4,3,2,1,0:T(8,128)(2,1)} %copy-done.2, ...), kind=kLoop, calls=%fused_computation.89 | loop fusion | flops 20969216 | bytes 13740032 | tf_op jit(solution)/shard_map/reduce_sum | solution.py:180
  76.6 2.8 %fusion.24 = f32[1,2,34,34,256]{4,3,2,1,0:T(8,128)S(1)} fusion(f32[1,2,32,32,256]{4,3,2,1,0:T(8,128)S(1)} %get-tuple-element.71, f32[256]{0:T(256)S(1)} %bitcast.181, f32[256]{0:T(256)S(1)} %bitcast.183, f32[256]{0:T(256)S(1)} %bitcast.169, f32[256]{0:T(256)S(1)} %bitcast.171, f32[256]{0:T(256)S(1)} %bitcast.173, f32[256]{0:T(256)S(1)} %bitcast.175, ...), kind=kLoop, calls=%fused_computation.48 | loop fusion | flops 10061824 | bytes 4473856 | tf_op jit(solution)/shard_map/add | solution.py:179
  80.9 2.3 fusion.91
  83.2 2.2 fusion.90
  87.0 41.3 %all-reduce.1 = (f32[256,9]{0,1:T(8,128)S(1)}, f32[256]{0:T(256)}, f32[1024]{0:T(1024)S(1)}, f32[256]{0:T(256)}) all-reduce(f32[256,9]{0,1:T(8,128)S(1)} %stack.109, f32[256]{0:T(256)S(1)} %get-tuple-element.57, f32[1024]{0:T(1024)S(1)} %copy-done.14, f32[256]{0:T(256)} %get-tuple-element.82), channel_id=1, replica_groups=mesh['tile'=4,'rep'=8] {'tile','rep'}, use_global_device_ids=true, to_apply=%region_13.14 | all-reduce | flops 3840 | bytes 30720 | tf_op jit(solution)/shard_map/psum | solution.py:234
  130.5 7.7 %all_gather.11 = bf16[1,8,4,32,256]{4,3,2,0,1:T(8,128)(2,1)S(1)} all-gather(bf16[1,2,4,32,256]{4,3,2,0,1:T(8,128)(2,1)S(1)} %copy.268), channel_id=1, replica_groups=mesh['tile'=4,'rep'=8] {'tile'}, dimensions={1}, use_global_device_ids=true | all-gather | bytes 655360 | tf_op jit(solution)/shard_map/all_gather | solution.py:218
  138.2 1.1 bitcast_convert_fusion
  139.3 2.5 %gather_fusion.2 = f32[8,32,256]{2,1,0:T(8,128)} fusion(f32[8,4,32,256]{3,2,1,0:T(8,128)} %bitcast_convert_fusion, s32[8]{0:T(128)S(1)} %reshape.574), kind=kCustom, calls=%fused_computation.2 | custom fusion | bytes 524352 | tf_op jit(solution)/shard_map/gather | solution.py:52
  141.8 1.6 rev.43
  143.5 1.1 broadcast_select_fusion
  145.9 1.2 broadcast_multiply_fusion.7
  150.2 1.4 collective-permute-done.1
  152.3 4.5 %fusion.56 = f32[1,2,32,32,256]{4,3,2,1,0:T(8,128)} fusion(f32[1,2,34,34,256]{4,3,2,1,0:T(8,128)S(1)} %fusion.24, bf16[1,2,32,32,256]{4,3,2,1,0:T(8,128)(2,1)} %param.11, f32[2,256]{1,0:T(2,128)S(1)} %bitcast.184, f32[2,256]{1,0:T(2,128)S(1)} %bitcast.185, f32[2,256]{1,0:T(2,128)S(1)} %bitcast.186, f32[2,256]{1,0:T(2,128)S(1)} %bitcast.187, ...), kind=kLoop, calls=%fused_computation.98 | loop fusion | flops 9437184 | bytes 5528576 | tf_op jit(solution)/shard_map/add | solution.py:108
  156.9 64.4 %all-reduce.5.cloned.1.call-done = (f32[256,1024]{1,0:T(8,128)}, f32[1024,256]{1,0:T(8,128)}) async-done(((f32[256,1024]{1,0:T(8,128)}, f32[1024,256]{1,0:T(8,128)}), (f32[256,1024]{1,0:T(8,128)}, f32[1024,256]{1,0:T(8,128)})) %all-reduce.5.cloned.1.call-update) | async-done | bytes 2097168 | tf_op jit(solution)/shard_map/psum | solution.py:234
  221.3 2.4 %broadcast_multiply_fusion = f32[1024,256]{1,0:T(8,128)} fusion(f32[1024,256]{1,0:T(8,128)} %get-tuple-element.70), kind=kLoop, calls=%fused_computation.118 | loop fusion | flops 262144 | bytes 2097152 | tf_op jit(solution)/shard_map/mul | solution.py:244
  (133 shorter events, 20.6 us)
Async XLA Ops:
  7.2 29.6 %copy-start = (bf16[256,1024]{1,0:T(8,128)(2,1)S(1)}, bf16[256,1024]{1,0:T(8,128)(2,1)}, u32[]{:S(2)}) copy-start(bf16[256,1024]{1,0:T(8,128)(2,1)} %param.16) | copy-start | bytes 1572868
  7.2 21.2 %copy-start.4 = (bf16[1,2,32,32,256]{4,3,2,1,0:T(8,128)(2,1)S(1)}, bf16[1,2,32,32,256]{4,3,2,1,0:T(8,128)(2,1)}, u32[]{:S(2)}) copy-start(bf16[1,2,32,32,256]{4,3,2,1,0:T(8,128)(2,1)} %param.10) | copy-start | bytes 3145732
  7.2 21.1 %copy-start.13 = (f32[256,9]{0,1:T(8,128)S(1)}, f32[256,9]{0,1:T(8,128)}, u32[]{:S(2)}) copy-start(f32[256,9]{0,1:T(8,128)} %param.14) | copy-start | bytes 27652
  7.2 214.1 %all-reduce.5.cloned.1.call-start = ((), (), s32[]{:S(2)}) async-start(), calls=%async_computation | async-start | bytes 4194304 | tf_op jit(solution)/shard_map/psum | solution.py:234
  11.4 16.5 %copy-start.15 = (pred[2,4]{1,0:T(4,128)(4,1)}, pred[2,4]{1,0:T(4,128)(4,1)S(1)}, u32[]{:S(2)}) copy-start(pred[2,4]{1,0:T(4,128)(4,1)S(1)} %compare_bitcast_fusion) | copy-start | bytes 28
  30.1 5.2 %copy-start.1 = (bf16[1,2,33,34,256]{4,3,2,1,0:T(8,128)(2,1)}, bf16[1,2,33,34,256]{4,3,2,1,0:T(8,128)(2,1)S(1)}, u32[]{:S(2)}) copy-start(bf16[1,2,33,34,256]{4,3,2,1,0:T(8,128)(2,1)S(1)} %get-tuple-element.84) | copy-start | bytes 3446788
  30.1 5.2 %copy-start.2 = (bf16[1,2,33,34,256]{4,3,2,1,0:T(8,128)(2,1)}, bf16[1,2,33,34,256]{4,3,2,1,0:T(8,128)(2,1)S(1)}, u32[]{:S(2)}) copy-start(bf16[1,2,33,34,256]{4,3,2,1,0:T(8,128)(2,1)S(1)} %get-tuple-element.85) | copy-start | bytes 3446788
  30.1 5.9 %copy-start.10 = (f32[256]{0:T(256)S(1)}, f32[256]{0:T(256)}, u32[]{:S(2)}) copy-start(f32[256]{0:T(256)} %param.15) | copy-start | bytes 3076
  36.7 19.4 %copy-start.8 = (bf16[1,2,32,32,256]{4,3,2,1,0:T(8,128)(2,1)}, bf16[1,2,32,32,256]{4,3,2,1,0:T(8,128)(2,1)S(1)}, u32[]{:S(2)}) copy-start(bf16[1,2,32,32,256]{4,3,2,1,0:T(8,128)(2,1)S(1)} %multiply_convert_fusion) | copy-start | bytes 3145732
  36.8 19.4 %copy-start.5 = (bf16[1,2,32,32,256]{4,3,2,1,0:T(8,128)(2,1)S(1)}, bf16[1,2,32,32,256]{4,3,2,1,0:T(8,128)(2,1)}, u32[]{:S(2)}) copy-start(bf16[1,2,32,32,256]{4,3,2,1,0:T(8,128)(2,1)} %param.10) | copy-start | bytes 3145732
  36.8 19.4 %copy-start.6 = (bf16[1,2,32,32,256]{4,3,2,1,0:T(8,128)(2,1)S(1)}, bf16[1,2,32,32,256]{4,3,2,1,0:T(8,128)(2,1)}, u32[]{:S(2)}) copy-start(bf16[1,2,32,32,256]{4,3,2,1,0:T(8,128)(2,1)} %param.11) | copy-start | bytes 3145732
  36.8 19.4 %copy-start.18 = (bf16[1024,256]{1,0:T(8,128)(2,1)S(1)}, bf16[1024,256]{1,0:T(8,128)(2,1)}, u32[]{:S(2)}) copy-start(bf16[1024,256]{1,0:T(8,128)(2,1)} %param.18) | copy-start | bytes 1572868
  36.8 19.4 %copy-start.20 = (f32[256]{0:T(256)S(1)}, f32[256]{0:T(256)}, u32[]{:S(2)}) copy-start(f32[256]{0:T(256)} %param.19) | copy-start | bytes 3076
  56.2 3.2 %copy-start.23 = (bf16[2048,1024]{1,0:T(8,128)(2,1)}, bf16[2048,1024]{1,0:T(8,128)(2,1)S(1)}, u32[]{:S(2)}) copy-start(bf16[2048,1024]{1,0:T(8,128)(2,1)S(1)} %get-tuple-element.128) | copy-start | bytes 12582916
  59.3 5.5 %copy-start.25 = (bf16[2048,256]{1,0:T(8,128)(2,1)}, bf16[2048,256]{1,0:T(8,128)(2,1)S(1)}, u32[]{:S(2)}) copy-start(bf16[2048,256]{1,0:T(8,128)(2,1)S(1)} %get-tuple-element.86) | copy-start | bytes 3145732
  68.1 12.8 %copy-start.26 = (bf16[2048,256]{1,0:T(8,128)(2,1)S(1)}, bf16[2048,256]{1,0:T(8,128)(2,1)}, u32[]{:S(2)}) copy-start(bf16[2048,256]{1,0:T(8,128)(2,1)} %copy-done.25) | copy-start | bytes 3145732
  76.6 4.4 %copy-start.24 = (bf16[2048,1024]{1,0:T(8,128)(2,1)S(1)}, bf16[2048,1024]{1,0:T(8,128)(2,1)}, u32[]{:S(2)}) copy-start(bf16[2048,1024]{1,0:T(8,128)(2,1)} %copy-done.23) | copy-start | bytes 12582916
  80.6 2.6 %copy-start.22 = (bf16[2048,1024]{1,0:T(8,128)(2,1)S(1)}, bf16[2048,1024]{1,0:T(8,128)(2,1)}, u32[]{:S(2)}) copy-start(bf16[2048,1024]{1,0:T(8,128)(2,1)} %copy-done.21) | copy-start | bytes 12582916
  80.6 66.6 %collective-permute-start = (bf16[1,1,2,4,256]{4,3,2,1,0:T(4,128)(2,1)}, bf16[1,1,2,4,256]{4,3,2,1,0:T(4,128)(2,1)}, u32[]{:S(2)}, u32[]{:S(2)}) collective-permute-start(bf16[1,1,2,4,256]{4,3,2,1,0:T(4,128)(2,1)} %pad_maximum_fusion.8), channel_id=1, source_target_pairs={{0,8},{8,0},{16,24},{24,16},{1,9},{9,1},{17,25},{25,17},{2,10},{10... | collective-permute-start | bytes 12296 | tf_op jit(solution)/shard_map/ppermute | solution.py:22
  86.1 57.3 %copy-start.16 = (pred[2,4]{1,0:T(4,128)(4,1)S(1)}, pred[2,4]{1,0:T(4,128)(4,1)}, u32[]{:S(2)}) copy-start(pred[2,4]{1,0:T(4,128)(4,1)} %copy-done.15) | copy-start | bytes 28
  86.9 58.4 %copy-start.11 = (pred[32]{0:T(512)(128)(4,1)}, pred[32]{0:T(512)(128)(4,1)S(1)}, u32[]{:S(2)}) copy-start(pred[32]{0:T(512)(128)(4,1)S(1)} %get-tuple-element.138) | copy-start | bytes 100
  86.9 58.4 %copy-start.12 = (pred[32]{0:T(512)(128)(4,1)}, pred[32]{0:T(512)(128)(4,1)S(1)}, u32[]{:S(2)}) copy-start(pred[32]{0:T(512)(128)(4,1)S(1)} %get-tuple-element.139) | copy-start | bytes 100
  129.6 19.2 %copy-start.17 = (f32[256]{0:T(256)S(1)}, f32[256]{0:T(256)}, u32[]{:S(2)}) copy-start(f32[256]{0:T(256)} %get-tuple-element.66) | copy-start | bytes 3076
  147.9 3.7 %collective-permute-start.1 = (bf16[2,1,2,4,256]{4,3,2,0,1:T(4,128)(2,1)S(1)}, bf16[2,1,2,4,256]{4,3,2,0,1:T(4,128)(2,1)S(1)}, u32[]{:S(2)}, u32[]{:S(2)}) collective-permute-start(bf16[2,1,2,4,256]{4,3,2,0,1:T(4,128)(2,1)S(1)} %get-tuple-element.117), channel_id=1, source_target_pairs={{0,16},{8,24},{16,0},{24,8},{1,17},{9,25},{17,1},{25,9},{2,18},{10... | collective-permute-start | bytes 24584 | tf_op jit(solution)/shard_map/ppermute | solution.py:22
  (6 other events, 11.1 us)
Sparse Core Ops, SparseCore 0:
  85.6 135.6 all-reduce.4
